TPU v7x, 32 devices: a whole 2x2x4 slice. The times are simulated.
32 devices in a mesh: grp: 2 (over y), blk: 16 (over z, x, core).
Axes of the slice: x: 2, y: 2, z: 4, core: 2. Of those that a mesh axis runs over, the one named last changes fastest.
Arguments:
- inputs: bfloat16 [8192, 768], P(('grp', 'blk')), may hold values from -6 to 6
- first_values: bfloat16 [8192, 384], P(('grp', 'blk')), may hold values from -6 to 6
- spans: int32 [2, 3], P('grp'), may hold values from 0 to 127, as said below
- ln1_gain: float32 [768], replicated, may hold values from 0.1 to 1.9
- ln1_shift: float32 [768], replicated, may hold values from -3 to 3
- w_query: bfloat16 [768, 768], replicated, may hold values from -0.5 to 0.5
- b_query: float32 [768], replicated, may hold values from -3 to 3
- w_key: bfloat16 [768, 768], replicated, may hold values from -0.21875 to 0.21875
- w_value: bfloat16 [768, 384], replicated, may hold values from -0.21875 to 0.21875
- b_value: float32 [384], replicated, may hold values from -3 to 3
- w_out: bfloat16 [768, 768], replicated, may hold values from -0.4375 to 0.4375
- b_out: float32 [768], replicated, may hold values from -3 to 3
- ln2_gain: float32 [768], replicated, may hold values from 0.1 to 1.9
- ln2_shift: float32 [768], replicated, may hold values from -3 to 3
- w_up: bfloat16 [768, 3072], replicated, may hold values from -0.21875 to 0.21875
- b_up: float32 [3072], replicated, may hold values from -3 to 3
- w_down: bfloat16 [3072, 768], replicated, may hold values from -0.109375 to 0.109375
- b_down: float32 [768], replicated, may hold values from -3 to 3
- out_grad: bfloat16 [8192, 768], P(('grp', 'blk')), may hold values from -6 to 6
Outputs:
- result: float32 [8192, 768], P(('grp', 'blk'))
- grad_inputs: float32 [8192, 768], P(('grp', 'blk'))
- grad_first_values: bfloat16 [8192, 384], P(('grp', 'blk'))
- grad_ln1_gain: float32 [768], replicated
- grad_ln1_shift: float32 [768], replicated
- grad_w_query: float32 [768, 768], P('blk')
- grad_b_query: float32 [768], replicated
- grad_w_key: float32 [768, 768], P('blk')
- grad_w_value: float32 [768, 384], P('blk')
- grad_b_value: float32 [384], replicated
- grad_w_out: float32 [768, 768], P('blk')
- grad_b_out: float32 [768], replicated
- grad_ln2_gain: float32 [768], replicated
- grad_ln2_shift: float32 [768], replicated
- grad_w_up: float32 [768, 3072], P('blk')
- grad_b_up: float32 [3072], replicated
- grad_w_down: float32 [3072, 768], P('blk')
- grad_b_down: float32 [768], replicated
Inputs may be any that keep to these rules, and one draw needn't show every extreme that they name: `spans`: each column lies in 0 .. 127, so one long document of each group runs from the first device of blk to the last; documents before and after it lie on the end devices.
All inputs are finite; a program needn't handle non-finite values.
Results may differ from a plain program's by a relative error of at most 0.02.
Values may be sent and summed in bfloat16 or wider, within the bound.
A program may use at most 192 MiB of HBM per device.

v0:
```python
import math

import jax
import jax.numpy as jnp
from jax import lax
from jax.sharding import PartitionSpec as P

HEADS = 12


EPSILON = 1e-05
GELU_COEF = 0.7978845608028654
NEG_FILL = -1e30


def layer_norm(values, gain_vector, shift_vector):
    average = jnp.mean(values, axis=-1, keepdims=True)
    centred = values - average
    variance = jnp.mean(centred * centred, axis=-1, keepdims=True)
    return centred * lax.rsqrt(variance + EPSILON) * gain_vector + shift_vector


def gelu_tanh(values):
    return (
        0.5 * values * (1.0 + jnp.tanh(GELU_COEF * (values + 0.044715 * values * values * values)))
    )


def key_alive(key_pos, bounds):
    return (key_pos < bounds[2]) | (key_pos >= bounds[1])


def allowed_mask(query_pos, key_pos, bounds):
    query_doc = (query_pos >= bounds[0]).astype(jnp.int32) + (query_pos >= bounds[1]).astype(
        jnp.int32
    )
    key_doc = (key_pos >= bounds[0]).astype(jnp.int32) + (key_pos >= bounds[1]).astype(jnp.int32)
    same_doc = query_doc[:, None] == key_doc[None, :]
    causal = key_pos[None, :] <= query_pos[:, None]
    return same_doc & causal & key_alive(key_pos, bounds)[None, :]


def block_grads(
    query_block,
    grad_block,
    lse_block,
    delta_block,
    query_pos,
    key_block,
    value_block,
    key_pos,
    bounds,
):
    allowed = allowed_mask(query_pos, key_pos, bounds)[None]
    scores = jnp.einsum("qhd,khd->hqk", query_block, key_block, preferred_element_type=jnp.float32)
    masked = jnp.where(allowed, scores, NEG_FILL)
    probabilities = jnp.where(allowed, jnp.exp(masked - jnp.transpose(lse_block)[:, :, None]), 0.0)
    prob_grads = jnp.einsum(
        "qhd,khd->hqk", grad_block, value_block, preferred_element_type=jnp.float32
    )
    score_grads = (probabilities * (prob_grads - jnp.transpose(delta_block)[:, :, None])).astype(
        jnp.bfloat16
    )
    return (probabilities.astype(jnp.bfloat16), score_grads)


def keep_state(carried):
    return carried


def body(
    inputs,
    first_values,
    spans,
    ln1_gain,
    ln1_shift,
    w_query,
    b_query,
    w_key,
    w_value,
    b_value,
    w_out,
    b_out,
    ln2_gain,
    ln2_shift,
    w_up,
    b_up,
    w_down,
    b_down,
    out_grad,
):
    row_count = inputs.shape[0]
    model_width = inputs.shape[1]
    half_width = model_width // 2
    head_count = HEADS
    head_size = model_width // head_count
    block_count = lax.axis_size("blk")
    length = row_count * block_count
    my_index = lax.axis_index("blk")
    start_row = my_index * row_count
    positions = start_row + jnp.arange(row_count, dtype=jnp.int32)
    last_pos = start_row + row_count - 1
    long_end = length - spans[0, 1]
    bounds = (spans[0, 0], long_end, long_end - spans[0, 2])
    source = inputs.astype(jnp.float32)
    normed, ln1_back = jax.vjp(layer_norm, source, ln1_gain, ln1_shift)
    normed_low = normed.astype(jnp.bfloat16)
    query_low = (
        (jnp.dot(normed_low, w_query, preferred_element_type=jnp.float32) + b_query) * 0.125
    ).astype(jnp.bfloat16)
    key_low = jnp.dot(normed_low, w_key, preferred_element_type=jnp.float32).astype(jnp.bfloat16)
    fresh_low = (jnp.dot(normed_low, w_value, preferred_element_type=jnp.float32) + b_value).astype(
        jnp.bfloat16
    )
    value_low = jnp.concatenate([fresh_low, first_values], axis=1)
    query_heads = query_low.reshape(row_count, head_count, head_size)
    key_heads = key_low.reshape(row_count, head_count, head_size)
    value_heads = value_low.reshape(row_count, head_count, head_size)
    start_state = (
        jnp.full((head_count, row_count), NEG_FILL, jnp.float32),
        jnp.zeros((head_count, row_count), jnp.float32),
        jnp.zeros((row_count, head_count, head_size), jnp.float32),
    )
    key_piece = lax.all_gather(key_low, "blk", axis=0, tiled=True)
    value_piece = lax.all_gather(value_low, "blk", axis=0, tiled=True)
    piece_rows = key_piece.shape[0]
    sub_rows = math.gcd(piece_rows, 512)

    def forward_one_block(block_index, carried):
        block_start = block_index * sub_rows

        def forward_compute(inner):
            row_max, row_total, accumulated = inner
            key_block = lax.dynamic_slice_in_dim(
                key_piece, block_index * sub_rows, sub_rows, 0
            ).reshape(sub_rows, head_count, head_size)
            value_block = lax.dynamic_slice_in_dim(
                value_piece, block_index * sub_rows, sub_rows, 0
            ).reshape(sub_rows, head_count, head_size)
            key_pos = block_start + jnp.arange(sub_rows, dtype=jnp.int32)
            allowed = allowed_mask(positions, key_pos, bounds)[None]
            scores = jnp.einsum(
                "qhd,khd->hqk", query_heads, key_block, preferred_element_type=jnp.float32
            )
            masked = jnp.where(allowed, scores, NEG_FILL)
            new_max = jnp.maximum(row_max, jnp.max(masked, axis=-1))
            unscaled = jnp.where(allowed, jnp.exp(masked - new_max[:, :, None]), 0.0)
            rescale = jnp.exp(row_max - new_max)
            new_total = row_total * rescale + jnp.sum(unscaled, axis=-1)
            new_acc = accumulated * jnp.transpose(rescale)[:, :, None] + jnp.einsum(
                "hqk,khd->qhd",
                unscaled.astype(jnp.bfloat16),
                value_block,
                preferred_element_type=jnp.float32,
            )
            return (new_max, new_total, new_acc)

        return lax.cond(block_start <= last_pos, forward_compute, keep_state, carried)

    row_max, row_total, accumulated = lax.fori_loop(
        0, piece_rows // sub_rows, forward_one_block, start_state
    )
    lse_rows = jnp.transpose(row_max + jnp.log(row_total))
    mixed = accumulated / jnp.transpose(row_total)[:, :, None]
    attended_low = mixed.reshape(row_count, model_width).astype(jnp.bfloat16)
    hidden = source + jnp.dot(attended_low, w_out, preferred_element_type=jnp.float32) + b_out
    normed2, ln2_back = jax.vjp(layer_norm, hidden, ln2_gain, ln2_shift)
    normed2_low = normed2.astype(jnp.bfloat16)
    upper = jnp.dot(normed2_low, w_up, preferred_element_type=jnp.float32) + b_up
    active, gelu_back = jax.vjp(gelu_tanh, upper)
    active_low = active.astype(jnp.bfloat16)
    result = hidden + jnp.dot(active_low, w_down, preferred_element_type=jnp.float32) + b_down
    alive_rows = key_alive(positions, bounds)
    grad_down = out_grad * alive_rows.astype(jnp.bfloat16)[:, None]
    g_w_down = jnp.einsum("tf,td->fd", active_low, grad_down, preferred_element_type=jnp.float32)
    g_b_down = jnp.sum(grad_down.astype(jnp.float32), axis=0)
    active_grad = jnp.einsum("td,fd->tf", grad_down, w_down, preferred_element_type=jnp.float32)
    upper_grad = gelu_back(active_grad)[0].astype(jnp.bfloat16)
    g_w_up = jnp.einsum("tc,tf->cf", normed2_low, upper_grad, preferred_element_type=jnp.float32)
    g_b_up = jnp.sum(upper_grad.astype(jnp.float32), axis=0)
    normed2_grad = jnp.einsum("tf,cf->tc", upper_grad, w_up, preferred_element_type=jnp.float32)
    hidden_norm_grad, g_ln2_gain, g_ln2_shift = ln2_back(normed2_grad)
    hidden_grad = grad_down.astype(jnp.float32) + hidden_norm_grad
    branch_grad = hidden_grad.astype(jnp.bfloat16)
    g_w_out = jnp.einsum("tc,td->cd", attended_low, branch_grad, preferred_element_type=jnp.float32)
    g_b_out = jnp.sum(branch_grad.astype(jnp.float32), axis=0)
    mixed_grad = jnp.einsum(
        "td,cd->tc", branch_grad, w_out, preferred_element_type=jnp.float32
    ).astype(jnp.bfloat16)
    grad_heads = mixed_grad.reshape(row_count, head_count, head_size)
    row_delta = jnp.sum(grad_heads.astype(jnp.float32) * mixed, axis=-1)
    zero_heads = jnp.zeros((row_count, head_count, head_size), jnp.float32)
    lse_all, delta_all = (
        lax.all_gather(lse_rows, "blk", axis=0, tiled=True),
        lax.all_gather(row_delta, "blk", axis=0, tiled=True),
    )
    key_key_piece = lax.all_gather(key_low, "blk", axis=0, tiled=True)
    key_value_piece = lax.all_gather(value_low, "blk", axis=0, tiled=True)
    piece_rows = key_key_piece.shape[0]
    key_sub_rows = math.gcd(piece_rows, 512)

    def key_one_block(block_index, carried):
        block_start = block_index * key_sub_rows

        def key_compute(inner):
            key_block = lax.dynamic_slice_in_dim(
                key_key_piece, block_index * key_sub_rows, key_sub_rows, 0
            ).reshape(key_sub_rows, head_count, head_size)
            value_block = lax.dynamic_slice_in_dim(
                key_value_piece, block_index * key_sub_rows, key_sub_rows, 0
            ).reshape(key_sub_rows, head_count, head_size)
            key_pos = block_start + jnp.arange(key_sub_rows, dtype=jnp.int32)
            unused, score_grads = block_grads(
                query_heads,
                grad_heads,
                lse_rows,
                row_delta,
                positions,
                key_block,
                value_block,
                key_pos,
                bounds,
            )
            return inner + jnp.einsum(
                "hqk,khd->qhd", score_grads, key_block, preferred_element_type=jnp.float32
            )

        return lax.cond(block_start <= last_pos, key_compute, keep_state, carried)

    query_grad = lax.fori_loop(0, piece_rows // key_sub_rows, key_one_block, zero_heads)
    query_piece = lax.all_gather(query_low, "blk", axis=0, tiled=True)
    grad_piece = lax.all_gather(mixed_grad, "blk", axis=0, tiled=True)
    piece_rows = query_piece.shape[0]
    query_sub_rows = math.gcd(piece_rows, 512)

    def query_one_block(block_index, carried):
        block_start = block_index * query_sub_rows

        def query_compute(inner):
            key_acc, value_acc = inner
            query_block = lax.dynamic_slice_in_dim(
                query_piece, block_index * query_sub_rows, query_sub_rows, 0
            ).reshape(query_sub_rows, head_count, head_size)
            grad_block = lax.dynamic_slice_in_dim(
                grad_piece, block_index * query_sub_rows, query_sub_rows, 0
            ).reshape(query_sub_rows, head_count, head_size)
            lse_block = lax.dynamic_slice_in_dim(lse_all, block_start, query_sub_rows, 0)
            delta_block = lax.dynamic_slice_in_dim(delta_all, block_start, query_sub_rows, 0)
            query_pos = block_start + jnp.arange(query_sub_rows, dtype=jnp.int32)
            prob_low, score_grads = block_grads(
                query_block,
                grad_block,
                lse_block,
                delta_block,
                query_pos,
                key_heads,
                value_heads,
                positions,
                bounds,
            )
            key_acc = key_acc + jnp.einsum(
                "hqk,qhd->khd", score_grads, query_block, preferred_element_type=jnp.float32
            )
            value_acc = value_acc + jnp.einsum(
                "hqk,qhd->khd", prob_low, grad_block, preferred_element_type=jnp.float32
            )
            return (key_acc, value_acc)

        return lax.cond(
            block_start + query_sub_rows - 1 >= start_row, query_compute, keep_state, carried
        )

    key_grad, value_grad = lax.fori_loop(
        0, piece_rows // query_sub_rows, query_one_block, (zero_heads, zero_heads)
    )
    scaled_grad = query_grad.reshape(row_count, model_width).astype(jnp.bfloat16) * jnp.bfloat16(
        0.125
    )
    key_grad_low = key_grad.reshape(row_count, model_width).astype(jnp.bfloat16)
    value_grad_low = value_grad.reshape(row_count, model_width).astype(jnp.bfloat16)
    fresh_grad = value_grad_low[:, :half_width]
    grad_first_values = value_grad_low[:, half_width:]
    g_w_query = jnp.einsum("tc,td->cd", normed_low, scaled_grad, preferred_element_type=jnp.float32)
    g_b_query = jnp.sum(scaled_grad.astype(jnp.float32), axis=0)
    g_w_key = jnp.einsum("tc,td->cd", normed_low, key_grad_low, preferred_element_type=jnp.float32)
    g_w_value = jnp.einsum("tc,td->cd", normed_low, fresh_grad, preferred_element_type=jnp.float32)
    g_b_value = jnp.sum(fresh_grad.astype(jnp.float32), axis=0)
    normed_grad = (
        jnp.einsum("td,cd->tc", scaled_grad, w_query, preferred_element_type=jnp.float32)
        + jnp.einsum("td,cd->tc", key_grad_low, w_key, preferred_element_type=jnp.float32)
        + jnp.einsum("td,cd->tc", fresh_grad, w_value, preferred_element_type=jnp.float32)
    )
    source_grad, g_ln1_gain, g_ln1_shift = ln1_back(normed_grad)
    grad_inputs = hidden_grad + source_grad
    vector_parts = (
        g_ln1_gain,
        g_ln1_shift,
        g_b_query,
        g_b_value,
        g_b_out,
        g_ln2_gain,
        g_ln2_shift,
        g_b_up,
        g_b_down,
    )
    vector_total = lax.psum(jnp.concatenate(vector_parts, axis=0), ("grp", "blk"))
    offsets = [0]
    for member in vector_parts:
        offsets.append(offsets[-1] + member.shape[0])
    summed_vectors = [
        vector_total[offsets[place] : offsets[place + 1]] for place in range(len(vector_parts))
    ]
    matrices = (g_w_query, g_w_key, g_w_value, g_w_out, g_w_up, g_w_down)
    shard_sums = (
        lax.psum_scatter(
            matrices[0].astype(jnp.bfloat16), "blk", scatter_dimension=0, tiled=True
        ).astype(jnp.float32),
        lax.psum_scatter(
            matrices[1].astype(jnp.bfloat16), "blk", scatter_dimension=0, tiled=True
        ).astype(jnp.float32),
        lax.psum_scatter(
            matrices[2].astype(jnp.bfloat16), "blk", scatter_dimension=0, tiled=True
        ).astype(jnp.float32),
        lax.psum_scatter(
            matrices[3].astype(jnp.bfloat16), "blk", scatter_dimension=0, tiled=True
        ).astype(jnp.float32),
        lax.psum_scatter(
            matrices[4].astype(jnp.bfloat16), "blk", scatter_dimension=0, tiled=True
        ).astype(jnp.float32),
        lax.psum_scatter(
            matrices[5].astype(jnp.bfloat16), "blk", scatter_dimension=0, tiled=True
        ).astype(jnp.float32),
    )
    shard_sums = (
        lax.psum(shard_sums[0].astype(jnp.bfloat16), "grp").astype(jnp.float32),
        lax.psum(shard_sums[1].astype(jnp.bfloat16), "grp").astype(jnp.float32),
        lax.psum(shard_sums[2].astype(jnp.bfloat16), "grp").astype(jnp.float32),
        lax.psum(shard_sums[3].astype(jnp.bfloat16), "grp").astype(jnp.float32),
        lax.psum(shard_sums[4].astype(jnp.bfloat16), "grp").astype(jnp.float32),
        lax.psum(shard_sums[5].astype(jnp.bfloat16), "grp").astype(jnp.float32),
    )
    return (
        result,
        grad_inputs,
        grad_first_values,
        summed_vectors[0],
        summed_vectors[1],
        shard_sums[0],
        summed_vectors[2],
        shard_sums[1],
        shard_sums[2],
        summed_vectors[3],
        shard_sums[3],
        summed_vectors[4],
        summed_vectors[5],
        summed_vectors[6],
        shard_sums[4],
        summed_vectors[7],
        shard_sums[5],
        summed_vectors[8],
    )


def solution(mesh):
    placed = (
        P(("grp", "blk"), None),
        P(("grp", "blk"), None),
        P("grp", None),
        P(),
        P(),
        P(),
        P(),
        P(),
        P(),
        P(),
        P(),
        P(),
        P(),
        P(),
        P(),
        P(),
        P(),
        P(),
        P(("grp", "blk"), None),
    )
    return jax.shard_map(
        body,
        mesh=mesh,
        in_specs=placed,
        out_specs=(
            P(("grp", "blk"), None),
            P(("grp", "blk"), None),
            P(("grp", "blk"), None),
            P(),
            P(),
            P("blk", None),
            P(),
            P("blk", None),
            P("blk", None),
            P(),
            P("blk", None),
            P(),
            P(),
            P(),
            P("blk", None),
            P(),
            P("blk", None),
            P(),
        ),
        check_vma=False,
    )
```

profile of v0, /device:TPU:0, one launch (start us, length us, event | category | flops | bytes accessed | tf_op | source)
XLA Modules:
  0.0 790.8 jit_solution(10757436689895299635)
XLA Ops:
  9.9 2.8 convolution_convert_fusion.7
  19.6 57.8 %all-gather.5.cloned.1.call-done = bf16[4096,768]{1,0:T(8,128)(2,1)} async-done(((bf16[256,768]{1,0:T(8,128)(2,1)}), bf16[4096,768]{1,0:T(8,128)(2,1)}) %all-gather.5.cloned.1.call-update) | async-done | bytes 6291472 | tf_op jit(solution)/shard_map/all_gather | solution.py:124
  77.4 8.6 %copy.50 = bf16[4096,768]{0,1:T(8,128)(2,1)} copy(bf16[4096,768]{1,0:T(8,128)(2,1)} %all-gather.5.cloned.1.call-done) | data formatting | bytes 12582912
  86.0 54.2 %all-gather.7.cloned.1.call-done = bf16[4096,768]{1,0:T(8,128)(2,1)} async-done(((bf16[256,768]{1,0:T(8,128)(2,1)}), bf16[4096,768]{1,0:T(8,128)(2,1)}) %all-gather.7.cloned.1.call-update) | async-done | bytes 6291472 | tf_op jit(solution)/shard_map/all_gather | solution.py:125
  140.2 8.7 %copy.51 = bf16[4096,768]{0,1:T(8,128)(2,1)} copy(bf16[4096,768]{1,0:T(8,128)(2,1)} %all-gather.7.cloned.1.call-done) | data formatting | bytes 12582912
  148.9 7.6 while.56
  149.0 7.2 conditional.10
  157.7 4.7 convolution_add_fusion
  162.4 4.9 convert_reduce_fusion
  174.2 1.9 copy.56
  178.3 14.3 %while.57 = (s32[]{:T(128)}, f32[256,12,64]{0,2,1:T(8,128)}, s32[]{:T(128)}, bf16[4096,768]{0,1:T(8,128)(2,1)}, s32[]{:T(128)}, /*index=5*/s32[]{:T(128)}, s32[]...) while((s32[]{:T(128)}, f32[256,12,64]{0,2,1:T(8,128)}, ...), condition=%wide.region_16.17_spmd.clone, body=%wide.region_13.16_spmd.clone.sunk | while | flops 614144512 | bytes 20749692 | solution.py:230
  178.3 14.1 %conditional.11 = (f32[256,12,64]{0,2,1:T(8,128)}) conditional(s32[]{:T(128)} %convert_element_type.396, f32[256,12,64]{0,2,1:T(8,128)} %get-tuple-element.1705, (s32[]{:T(128)}, bf16[4096,768]{0,1:T(8,128)(2,1)}, s32[]{:T(128)}, s32[]{:T(128)}, s32[]{:T(128)}, /*index=5*/s32[]{:T(128)}, s32[]{:T(128)}, bf16[256,12,64]{2,1,0:T(8,128)(2,1)S(1)}, ...), branch_computations={%region_14.14_spmd, %region_15.15_spmd} | conditional | flops 614144512 | bytes 20748382 | solution.py:228
  179.8 3.7 fusion.43
  185.0 7.4 fusion.38
  197.5 5.2 convolution_convert_fusion.1
  203.7 6.4 convolution_convert_fusion
  211.4 1.9 copy.61
  213.3 8.6 %copy.59 = bf16[4096,768]{0,1:T(8,128)(2,1)} copy(bf16[4096,768]{1,0:T(8,128)(2,1)} %all-gather.9.cloned.1.call-done) | data formatting | bytes 12582912
  221.9 169.4 %all_gather.25 = f32[4096,12]{0,1:T(8,128)} all-gather(f32[256,12]{0,1:T(8,128)S(1)} %get-tuple-element.1853), channel_id=1, replica_groups=mesh['grp'=2,'blk'=16] {'blk'}, dimensions={0}, use_global_device_ids=true | all-gather | bytes 208896 | tf_op jit(solution)/shard_map/all_gather | solution.py:195
  391.3 19.6 %all_gather.23 = f32[4096,12]{0,1:T(8,128)} all-gather(f32[256,12]{0,1:T(8,128)S(1)} %bitcast.141), channel_id=1, replica_groups=mesh['grp'=2,'blk'=16] {'blk'}, dimensions={0}, use_global_device_ids=true | all-gather | bytes 208896 | tf_op jit(solution)/shard_map/all_gather | solution.py:194
  410.9 8.8 %copy.60 = bf16[4096,768]{0,1:T(8,128)(2,1)} copy(bf16[4096,768]{1,0:T(8,128)(2,1)} %all-gather.11.cloned.1.call-done) | data formatting | bytes 12582912
  420.7 165.3 %while.58 = (s32[]{:T(128)}, f32[256,12,64]{0,2,1:T(8,128)S(1)}, f32[256,12,64]{0,2,1:T(8,128)}, s32[]{:T(128)}, bf16[4096,768]{0,1:T(8,128)(2,1)}, /*index=5*/s...) while((s32[]{:T(128)}, f32[256,12,64]{0,2,1:T(8,128)S(1)}, ...), condition=%wide.region_20.21_spmd.clone.clone, body=%wide.region_17.20_spmd.clone.clone.sunk | while | flops 821957888 | bytes 35971088 | solution.py:273
  420.7 20.6 %conditional.12 = ((f32[256,12,64]{0,2,1:T(8,128)S(1)}, f32[256,12,64]{0,2,1:T(8,128)})) conditional(s32[]{:T(128)} %convert_element_type.397, (f32[256,12,64]{0,2,1:T(8,128)S(1)}, f32[256,12,64]{0,2,1:T(8,128)}) %tuple.184, (s32[]{:T(128)}, bf16[4096,768]{0,1:T(8,128)(2,1)}, s32[]{:T(128)}, s32[]{:T(128)}, s32[]{:T(128)}, /*index=5*/s32[]{:T(128)}, ...), branch_computations={%region_18.18_spmd, %region_19.19_spmd} | conditional | flops 821957888 | bytes 35969736 | solution.py:269
  423.1 3.6 fusion.123
  429.0 7.2 fusion.64
  436.3 5.0 fusion.65
  441.3 20.4 %conditional.12 = ((f32[256,12,64]{0,2,1:T(8,128)S(1)}, f32[256,12,64]{0,2,1:T(8,128)})) conditional(s32[]{:T(128)} %convert_element_type.397, (f32[256,12,64]{0,2,1:T(8,128)S(1)}, f32[256,12,64]{0,2,1:T(8,128)}) %tuple.184, (s32[]{:T(128)}, bf16[4096,768]{0,1:T(8,128)(2,1)}, s32[]{:T(128)}, s32[]{:T(128)}, s32[]{:T(128)}, /*index=5*/s32[]{:T(128)}, ...), branch_computations={%region_18.18_spmd, %region_19.19_spmd} | conditional | flops 821957888 | bytes 35969736 | solution.py:269
  443.6 3.6 fusion.123
  449.6 7.1 fusion.64
  456.7 5.0 fusion.65
  461.7 21.1 %conditional.12 = ((f32[256,12,64]{0,2,1:T(8,128)S(1)}, f32[256,12,64]{0,2,1:T(8,128)})) conditional(s32[]{:T(128)} %convert_element_type.397, (f32[256,12,64]{0,2,1:T(8,128)S(1)}, f32[256,12,64]{0,2,1:T(8,128)}) %tuple.184, (s32[]{:T(128)}, bf16[4096,768]{0,1:T(8,128)(2,1)}, s32[]{:T(128)}, s32[]{:T(128)}, s32[]{:T(128)}, /*index=5*/s32[]{:T(128)}, ...), branch_computations={%region_18.18_spmd, %region_19.19_spmd} | conditional | flops 821957888 | bytes 35969736 | solution.py:269
  464.0 3.6 fusion.123
  470.0 7.4 fusion.64
  477.4 5.4 fusion.65
  482.8 20.5 %conditional.12 = ((f32[256,12,64]{0,2,1:T(8,128)S(1)}, f32[256,12,64]{0,2,1:T(8,128)})) conditional(s32[]{:T(128)} %convert_element_type.397, (f32[256,12,64]{0,2,1:T(8,128)S(1)}, f32[256,12,64]{0,2,1:T(8,128)}) %tuple.184, (s32[]{:T(128)}, bf16[4096,768]{0,1:T(8,128)(2,1)}, s32[]{:T(128)}, s32[]{:T(128)}, s32[]{:T(128)}, /*index=5*/s32[]{:T(128)}, ...), branch_computations={%region_18.18_spmd, %region_19.19_spmd} | conditional | flops 821957888 | bytes 35969736 | solution.py:269
  485.2 3.6 fusion.123
  491.2 7.1 fusion.64
  498.3 5.0 fusion.65
  503.2 20.5 %conditional.12 = ((f32[256,12,64]{0,2,1:T(8,128)S(1)}, f32[256,12,64]{0,2,1:T(8,128)})) conditional(s32[]{:T(128)} %convert_element_type.397, (f32[256,12,64]{0,2,1:T(8,128)S(1)}, f32[256,12,64]{0,2,1:T(8,128)}) %tuple.184, (s32[]{:T(128)}, bf16[4096,768]{0,1:T(8,128)(2,1)}, s32[]{:T(128)}, s32[]{:T(128)}, s32[]{:T(128)}, /*index=5*/s32[]{:T(128)}, ...), branch_computations={%region_18.18_spmd, %region_19.19_spmd} | conditional | flops 821957888 | bytes 35969736 | solution.py:269
  505.6 3.6 fusion.123
  511.6 7.2 fusion.64
  518.7 5.0 fusion.65
  523.8 20.6 %conditional.12 = ((f32[256,12,64]{0,2,1:T(8,128)S(1)}, f32[256,12,64]{0,2,1:T(8,128)})) conditional(s32[]{:T(128)} %convert_element_type.397, (f32[256,12,64]{0,2,1:T(8,128)S(1)}, f32[256,12,64]{0,2,1:T(8,128)}) %tuple.184, (s32[]{:T(128)}, bf16[4096,768]{0,1:T(8,128)(2,1)}, s32[]{:T(128)}, s32[]{:T(128)}, s32[]{:T(128)}, /*index=5*/s32[]{:T(128)}, ...), branch_computations={%region_18.18_spmd, %region_19.19_spmd} | conditional | flops 821957888 | bytes 35969736 | solution.py:269
  526.3 3.6 fusion.123
  532.3 7.1 fusion.64
  539.4 5.0 fusion.65
  544.4 21.2 %conditional.12 = ((f32[256,12,64]{0,2,1:T(8,128)S(1)}, f32[256,12,64]{0,2,1:T(8,128)})) conditional(s32[]{:T(128)} %convert_element_type.397, (f32[256,12,64]{0,2,1:T(8,128)S(1)}, f32[256,12,64]{0,2,1:T(8,128)}) %tuple.184, (s32[]{:T(128)}, bf16[4096,768]{0,1:T(8,128)(2,1)}, s32[]{:T(128)}, s32[]{:T(128)}, s32[]{:T(128)}, /*index=5*/s32[]{:T(128)}, ...), branch_computations={%region_18.18_spmd, %region_19.19_spmd} | conditional | flops 821957888 | bytes 35969736 | solution.py:269
  546.7 3.6 fusion.123
  552.7 7.5 fusion.64
  560.2 5.4 fusion.65
  565.6 20.4 %conditional.12 = ((f32[256,12,64]{0,2,1:T(8,128)S(1)}, f32[256,12,64]{0,2,1:T(8,128)})) conditional(s32[]{:T(128)} %convert_element_type.397, (f32[256,12,64]{0,2,1:T(8,128)S(1)}, f32[256,12,64]{0,2,1:T(8,128)}) %tuple.184, (s32[]{:T(128)}, bf16[4096,768]{0,1:T(8,128)(2,1)}, s32[]{:T(128)}, s32[]{:T(128)}, s32[]{:T(128)}, /*index=5*/s32[]{:T(128)}, ...), branch_computations={%region_18.18_spmd, %region_19.19_spmd} | conditional | flops 821957888 | bytes 35969736 | solution.py:269
  568.0 3.6 fusion.123
  573.9 7.1 fusion.64
  581.0 5.0 fusion.65
  588.1 6.3 fusion.83
  594.5 1.9 fusion.124
  600.9 18.6 %reduce-scatter.17.cloned.1.call-done = bf16[192,768]{1,0:T(8,128)(2,1)} async-done(((bf16[3072,768]{1,0:T(8,128)(2,1)}), bf16[192,768]{1,0:T(8,128)(2,1)}) %reduce-scatter.17.cloned.1.call-update) | async-done | bytes 294928 | tf_op jit(solution)/shard_map/reduce_scatter | solution.py:330
  619.6 60.7 %reduce-scatter.9.cloned.1.call-done = bf16[48,768]{1,0:T(8,128)(2,1)} async-done(((bf16[768,768]{1,0:T(8,128)(2,1)}), bf16[48,768]{1,0:T(8,128)(2,1)}) %reduce-scatter.9.cloned.1.call-update) | async-done | bytes 73744 | tf_op jit(solution)/shard_map/reduce_scatter | solution.py:318
  680.4 2.4 convert_reduce_fusion.2
  682.8 40.3 %psum.49 = f32[8832]{0:T(1024)S(1)} all-reduce(f32[8832]{0:T(1024)S(1)} %constant_dynamic-update-slice_fusion), channel_id=1, replica_groups=mesh['grp'=2,'blk'=16] {'grp','blk'}, use_global_device_ids=true, to_apply=%region_32.33 | all-reduce | flops 8832 | bytes 70656 | tf_op jit(solution)/shard_map/psum | solution.py:306
  725.8 12.3 %reduce-scatter.11.cloned.1.call-done = bf16[48,384]{1,0:T(8,128)(2,1)} async-done(((bf16[768,384]{1,0:T(8,128)(2,1)}), bf16[48,384]{1,0:T(8,128)(2,1)}) %reduce-scatter.11.cloned.1.call-update) | async-done | bytes 36880 | tf_op jit(solution)/shard_map/reduce_scatter | solution.py:321
  738.1 9.1 %psum.52 = bf16[48,384]{1,0:T(8,128)(2,1)S(1)} all-reduce(bf16[48,384]{1,0:T(8,128)(2,1)} %reduce-scatter.11.cloned.1.call-done), channel_id=1, replica_groups=mesh['grp'=2,'blk'=16] {'grp'}, use_global_device_ids=true, to_apply=%region_38.39 | all-reduce | flops 18432 | bytes 73728 | tf_op jit(solution)/shard_map/psum | solution.py:337
  747.9 27.7 %all-reduce.3.cloned.1.call-done = (bf16[48,768]{1,0:T(8,128)(2,1)}, bf16[48,768]{1,0:T(8,128)(2,1)}, bf16[48,768]{1,0:T(8,128)(2,1)}, bf16[48,3072]{1,0:T(8,128)(2,1)}, bf16[192,768]{1,0:T(8,128)(2,1)}) async-done(((bf16[48,768]{1,0:T(8,128)(2,1)}, bf16[48,768]{1,0:T(8,128)(2,1)}, bf16[48,768]{1,0:T(8,128)(2,1)}, bf16[48,3072]{1,0:T(8,128)(2,1)}, bf16[192,768]{1,0:T(8,128)(2,1)}), ...) | async-done | bytes 811024 | tf_op jit(solution)/shard_map/psum | solution.py:335
  780.2 1.8 convert_element_type.260
  (310 shorter events, 90.2 us)
Async XLA Ops:
  7.2 149.5 %copy-start = (bf16[768,768]{1,0:T(8,128)(2,1)S(1)}, bf16[768,768]{1,0:T(8,128)(2,1)}, u32[]{:S(2)}) copy-start(bf16[768,768]{1,0:T(8,128)(2,1)} %param.41) | copy-start | bytes 3538948
  7.2 5.5 copy-start.4
  7.2 5.5 copy-start.35
  7.2 5.5 copy-start.27
  7.2 5.5 copy-start.23
  7.3 5.5 copy-start.36
  7.3 70.1 %all-gather.5.cloned.1.call-start = ((), (), s32[]{:S(2)}) async-start(), calls=%async_computation.6 | async-start | bytes 6684672 | tf_op jit(solution)/shard_map/all_gather | solution.py:124
  9.8 6.6 copy-start.28
  9.8 5.2 copy-start.22
  9.8 5.2 copy-start.33
  12.7 127.5 %all-gather.7.cloned.1.call-start = ((), (), s32[]{:S(2)}) async-start(), calls=%async_computation.7 | async-start | bytes 6684672 | tf_op jit(solution)/shard_map/all_gather | solution.py:125
  13.3 4.4 copy-start.30
  15.0 198.3 %all-gather.9.cloned.1.call-start = ((), (), s32[]{:S(2)}) async-start(), calls=%async_computation.8 | async-start | bytes 6684672 | tf_op jit(solution)/shard_map/all_gather | solution.py:231
  16.4 394.5 %all-gather.11.cloned.1.call-start = ((), (), s32[]{:S(2)}) async-start(), calls=%async_computation.9 | async-start | bytes 6684672 | tf_op jit(solution)/shard_map/all_gather | solution.py:232
  148.9 7.8 copy-start.31
  156.6 5.8 copy-start.5
  156.6 1.0 copy-start.25
  156.6 1.0 copy-start.26
  156.6 1.0 copy-start.32
  156.7 5.7 copy-start.9
  156.7 5.7 slice-start.2
  157.3 11.7 %copy-start.2 = (f32[256,768]{1,0:T(8,128)}, f32[256,768]{1,0:T(8,128)S(1)}, u32[]{:S(2)}) copy-start(f32[256,768]{1,0:T(8,128)S(1)} %get-tuple-element.1391) | copy-start | bytes 2359300
  157.6 4.8 copy-start.15
  157.6 4.8 slice-start.3
  157.6 9.7 %slice-start = ((s8[4718592]{0:T(1024)(128)(4,1)}), s8[4194304]{0:T(1024)(128)(4,1)S(1)}, s32[]{:S(2)}) async-start(s8[4718592]{0:T(1024)(128)(4,1)} %bitcast.142), calls=%async_computation.17 | async-start | bytes 8388608
  162.4 4.9 copy-start.37
  162.4 4.9 slice-start.1
  167.3 1.7 copy-start.20
  169.4 0.9 copy-start.6
  170.5 6.8 copy-start.11
  171.8 429.0 %reduce-scatter.7.cloned.1.call-start = ((), (), s32[]{:S(2)}) async-start(), calls=%async_computation.10 | async-start | bytes 1253376 | tf_op jit(solution)/shard_map/reduce_scatter | solution.py:315
  192.7 3.2 copy-start.10
  192.7 3.2 copy-start.12
  194.1 3.3 copy-start.18
  194.1 3.4 copy-start.3
  195.9 405.0 %reduce-scatter.13.cloned.1.call-start = ((), (), s32[]{:S(2)}) async-start(), calls=%async_computation.13 | async-start | bytes 1253376 | tf_op jit(solution)/shard_map/reduce_scatter | solution.py:324
  197.5 403.5 %reduce-scatter.15.cloned.1.call-start = ((), (), s32[]{:S(2)}) async-start(), calls=%async_computation.14 | async-start | bytes 5013504 | tf_op jit(solution)/shard_map/reduce_scatter | solution.py:327
  202.7 1.0 copy-start.16
  202.7 416.8 %reduce-scatter.17.cloned.1.call-start = ((), (), s32[]{:S(2)}) async-start(), calls=%async_computation.15 | async-start | bytes 5013504 | tf_op jit(solution)/shard_map/reduce_scatter | solution.py:330
  210.1 1.0 copy-start.17
  210.1 1.2 copy-start.8
  210.1 470.2 %reduce-scatter.9.cloned.1.call-start = ((), (), s32[]{:S(2)}) async-start(), calls=%async_computation.11 | async-start | bytes 1253376 | tf_op jit(solution)/shard_map/reduce_scatter | solution.py:318
  436.3 5.0 copy-start.14
  441.3 0.9 copy-start.13
  456.7 5.0 copy-start.14
  477.4 5.4 copy-start.14
  482.8 0.9 copy-start.13
  498.2 5.0 copy-start.14
  503.2 0.9 copy-start.13
  518.7 5.0 copy-start.14
  523.8 0.9 copy-start.13
  539.4 5.0 copy-start.14
  544.4 0.9 copy-start.13
  560.2 5.4 copy-start.14
  581.0 5.0 copy-start.14
  586.0 2.1 copy-start.34
  587.8 6.7 copy-start.19
  587.8 150.3 %reduce-scatter.11.cloned.1.call-start = ((), (), s32[]{:S(2)}) async-start(), calls=%async_computation.12 | async-start | bytes 626688 | tf_op jit(solution)/shard_map/reduce_scatter | solution.py:321
  594.4 3.2 copy-start.21
  594.5 3.6 copy-start.24
  597.6 1.1 copy-start.29
  598.7 81.7 %copy-start.7 = (f32[256,768]{1,0:T(8,128)S(1)}, f32[256,768]{1,0:T(8,128)}, u32[]{:S(2)}) copy-start(f32[256,768]{1,0:T(8,128)} %copy-done.6) | copy-start | bytes 2359300
  600.6 175.0 %all-reduce.3.cloned.1.call-start = ((), (), s32[]{:S(2)}) async-start(), calls=%async_computation.16 | async-start | bytes 1622016 | tf_op jit(solution)/shard_map/psum | solution.py:335
  680.4 103.5 %copy-start.1 = (bf16[768,768]{1,0:T(8,128)(2,1)S(1)}, bf16[768,768]{1,0:T(8,128)(2,1)}, u32[]{:S(2)}) copy-start(bf16[768,768]{1,0:T(8,128)(2,1)} %param.41) | copy-start | bytes 3538948
  (3 other events, 2.6 us)
Sparse Core Ops, SparseCore 0:
  12.8 64.5 all-gather.4
  79.7 60.4 all-gather.6
  143.0 60.5 all-gather.8
  205.7 76.7 all-gather.10
  285.9 115.5 reduce-scatter.6
  405.0 57.0 reduce-scatter.12
  466.0 74.5 reduce-scatter.14
  545.0 74.5 reduce-scatter.16
  623.2 57.0 reduce-scatter.8
  684.3 53.7 reduce-scatter.10
  740.9 34.6 all-reduce.2
where the time goes:
time: 803 us; the launch traced here: 791 us
  blocking collectives  238 us (30%)
  waiting for transfers between devices  232 us (29%)
  matrix products  186 us (23%)
  local copies, waits for them, and re-layouts  78.5 us (10%)
  other arithmetic  37.5 us (5%)
  between operations  16.5 us (2%)
    all_gather x1, blocking collectives, body(): lax.all_gather(row_delta, 'blk', axis=0, tiled=True)  169 us
    reduce_scatter x1, waiting for transfers between devices, body(): lax.psum_scatter(matrices[1].astype(jnp.bfloat16), 'blk', scatter_dimensi...  60.7 us
    all_gather x1, waiting for transfers between devices, body(): key_piece = lax.all_gather(key_low, 'blk', axis=0, tiled=True)  57.8 us
    dot_general x8, matrix products, query_compute(): jnp.einsum('hqk,qhd->khd', score_grads, query_block, preferred_element_ty...  57.7 us
    all_gather x1, waiting for transfers between devices, body(): value_piece = lax.all_gather(value_low, 'blk', axis=0, tiled=True)  54.2 us
    unnamed x96, local copies, waits for them, and re-layouts  43 us
    dot_general x8, matrix products, query_compute(): jnp.einsum('hqk,qhd->khd', prob_low, grad_block, preferred_element_type=j...  40.6 us
    psum x1, blocking collectives, body(): lax.psum(jnp.concatenate(vector_parts, axis=0), ('grp', 'blk'))  40.3 us
  transfers between devices with their start and end apart: 11, of which 6 were waited for; matrix products, arithmetic and copies ran while one was open for 35% of the time, Pallas kernels for 0%

commit v1 on v0

v1 whole, which is shorter than its diff:
```python
import functools

import jax
import jax.numpy as jnp
from jax import lax
from jax.experimental import pallas as pl
from jax.experimental.pallas import tpu as pltpu
from jax.sharding import PartitionSpec as P

HEADS = 12
PLANES = 4
SLOTS = HEADS // PLANES
EPSILON = 1e-05
GELU_COEF = 0.7978845608028654
NEG_FILL = -1e30
BF16 = jnp.bfloat16
F32 = jnp.float32
MESH = pl.DeviceIdType.MESH
VMEM = pl.BlockSpec(memory_space=pltpu.VMEM)
SMEM = pl.BlockSpec(memory_space=pltpu.SMEM)


def dot(a, b, dims):
    return lax.dot_general(a, b, (dims, ((), ())), preferred_element_type=F32)


NN = ((1,), (0,))
NT = ((1,), (1,))
TN = ((0,), (0,))


def norm_rows(values, gain, shift):
    average = jnp.mean(values, axis=-1, keepdims=True)
    centred = values - average
    variance = jnp.mean(centred * centred, axis=-1, keepdims=True)
    return centred * lax.rsqrt(variance + EPSILON) * gain + shift


def place(plane):
    block = lax.axis_index("blk")
    return block // plane, lax.rem(block, plane)


def at_z(z, c, plane, offset):
    return {"blk": lax.rem(z + offset, PLANES) * plane + c}


def at_x(z, c, plane, offset):
    lines = plane // 2
    column, core = c // 2, lax.rem(c, 2)
    return {"blk": z * plane + lax.rem(column + offset, lines) * 2 + core}


def at_core(z, c, plane):
    return {"blk": z * plane + (c // 2) * 2 + 1 - lax.rem(c, 2)}


def greet(partners):
    barrier = pltpu.get_barrier_semaphore()
    for partner in partners:
        pl.semaphore_signal(barrier, inc=1, device_id=partner, device_id_type=MESH)
    pl.semaphore_wait(barrier, len(partners))


def remote(src, dst, send, recv, partner):
    return pltpu.make_async_remote_copy(
        src_ref=src, dst_ref=dst, send_sem=send, recv_sem=recv,
        device_id=partner, device_id_type=MESH,
    )


def query_rows(pack, first):
    half = pack.shape[1] // 2
    lanes = lax.broadcasted_iota(jnp.int32, pack.shape, 1)
    wide = pack.astype(F32)
    other = pltpu.roll(wide, half, 1)
    keep = lanes < half if first else lanes >= half
    top, bottom = (wide, other) if first else (other, wide)
    return jnp.concatenate(
        [jnp.where(keep, top, 0.0), jnp.where(keep, bottom, 0.0)], axis=0
    ).astype(BF16)


def position_masks(spans_ref, plane, length, c, k, rows):
    first, end = spans_ref[0, 0], length - spans_ref[0, 1]
    dead = end - spans_ref[0, 2]
    width = plane * rows
    key = k * width + lax.broadcasted_iota(jnp.int32, (width, rows), 0)
    query = k * width + c * rows + lax.broadcasted_iota(jnp.int32, (width, rows), 1)
    allowed = key <= query
    if k == 0:
        allowed &= ((key >= first) == (query >= first))
    if k == PLANES - 1:
        allowed &= ((key >= end) == (query >= end)) & ((key < dead) | (key >= end))
    return jnp.where(allowed, 0.0, NEG_FILL)


def forward_kernel(
    plane, x_ref, fv_ref, spans_ref, g_ref, s_ref, wq_ref, bq_ref, wk_ref, wv_ref, bv_ref,
    att_ref, normed_ref, all_ref, o_ref, lse_ref,
    pack, opack, orecv, masks,
    zsend, zrecv, xsend, xrecv, csend, crecv, osend, orecv_sem,
):
    rows, width = x_ref.shape
    size = width // HEADS
    lines = plane // 2
    length = rows * plane * PLANES
    half = rows // 2
    z, c = place(plane)
    core = lax.rem(c, 2)
    greet(
        [at_z(z, c, plane, d) for d in range(1, PLANES)]
        + [at_x(z, c, plane, d) for d in range(1, lines)]
        + [at_core(z, c, plane)]
    )
    normed = norm_rows(x_ref[...].astype(F32), g_ref[...], s_ref[...]).astype(BF16)
    normed_ref[...] = normed
    query = ((dot(normed, wq_ref[...], NN) + bq_ref[...]) * 0.125)
    key = dot(normed, wk_ref[...], NN)
    fresh = dot(normed, wv_ref[...], NN) + bv_ref[...]
    value = jnp.concatenate([fresh, fv_ref[...].astype(F32)], axis=1)
    for head in range(HEADS):
        to, slot = divmod(head, SLOTS)
        cols = slice(head * size, (head + 1) * size)
        pack[to, slot, :rows, :] = jnp.concatenate(
            [key[:, cols], value[:, cols]], axis=1
        ).astype(BF16)
        pack[to, slot, rows:, :] = jnp.concatenate(
            [query[:half, cols], query[half:, cols]], axis=1
        ).astype(BF16)

    zcopies = {}
    for slot in range(SLOTS):
        for d in (2, 1, 3):
            to = lax.rem(z + d, PLANES)
            copy = remote(
                pack.at[to, slot], all_ref.at[slot, z, c],
                zsend.at[slot, d], zrecv.at[slot, d], at_z(z, c, plane, d),
            )
            copy.start()
            zcopies[slot, d] = copy
        all_ref[slot, z, c] = pack[z, slot]

    for k in range(PLANES):
        masks[k] = position_masks(spans_ref, plane, length, c, k, rows)
    first, end = spans_ref[0, 0], length - spans_ref[0, 1]

    started = []

    def spread(slot):
        for d in (0, 1, 3, 2):
            src = lax.rem(z + PLANES - d, PLANES)
            if d:
                zcopies[slot, d].wait_recv()
            block = all_ref.at[slot, src, c, pl.ds(0, rows)]
            for e in range(1, lines):
                copy = remote(
                    block, block, xsend.at[slot, d, e], xrecv.at[slot, d, e], at_x(z, c, plane, e)
                )
                copy.start()
                started.append(copy)
            copy = remote(block, block, csend.at[slot, d, 0], crecv.at[slot, d, 0], at_core(z, c, plane))
            copy.start()
            started.append(copy)

    def pass_on(slot):
        for d in (0, 1, 3, 2):
            src = lax.rem(z + PLANES - d, PLANES)
            for e in range(1, lines):
                column = lax.rem(c // 2 + lines - e, lines) * 2 + core
                block = all_ref.at[slot, src, column, pl.ds(0, rows)]
                remote(
                    block, block, xsend.at[slot, d, e], xrecv.at[slot, d, e], at_x(z, c, plane, e)
                ).wait_recv()
                copy = remote(
                    block, block, csend.at[slot, d, e], crecv.at[slot, d, e], at_core(z, c, plane)
                )
                copy.start()
                started.append(copy)

    def settle(slot):
        for d in range(PLANES):
            for e in range(lines):
                block = all_ref.at[slot, 0, c, pl.ds(0, rows)]
                remote(
                    block, block, csend.at[slot, d, e], crecv.at[slot, d, e], at_core(z, c, plane)
                ).wait_recv()

    def keys_of(slot, k):
        return all_ref[slot, k, :, :rows, :].reshape(plane * rows, 2 * size)

    def attend(slot, k):
        q = query_rows(all_ref[slot, k, c, rows:, :], True)

        def step(state, k2, bias):
            top, total, acc = state
            keys = keys_of(slot, k2)
            scores = bias(dot(keys, q, NT))
            new = jnp.maximum(top, jnp.max(scores, axis=0, keepdims=True))
            prob = jnp.exp(scores - new)
            scale = jnp.exp(top - new)
            return (
                new,
                total * scale + jnp.sum(prob, axis=0, keepdims=True),
                acc * scale + dot(keys, prob.astype(BF16), TN),
            )

        state = (
            jnp.full((1, rows), NEG_FILL, F32),
            jnp.zeros((1, rows), F32),
            jnp.zeros((2 * size, rows), F32),
        )
        state = step(state, k, lambda t: t + masks[k])
        diagonal = state
        for k2 in range(k):
            if k2 == 0:
                index = lax.broadcasted_iota(jnp.int32, (plane * rows, 1), 0)
                shut = jnp.where(index < first, NEG_FILL, 0.0)
                state = step(state, k2, lambda t: t + shut)
            else:
                state = step(state, k2, lambda t: t)
        if k == PLANES - 1:
            position = k * plane * rows + c * rows + lax.broadcasted_iota(jnp.int32, (1, rows), 1)
            after = position >= end
            state = tuple(jnp.where(after, old, new) for old, new in zip(diagonal, state))
        top, total, acc = state
        mixed = acc[size:] / total
        o_ref[slot, k] = mixed
        lse_ref[slot, k] = jnp.broadcast_to(top + jnp.log(total), (8, rows))
        packed = jnp.concatenate([mixed[:, :half], mixed[:, half:]], axis=0)
        opack[slot, k] = jnp.transpose(packed).astype(BF16)

    def give_back(slot):
        orecv[slot, z] = opack[slot, z]
        for d in (2, 1, 3):
            to = lax.rem(z + d, PLANES)
            copy = remote(
                opack.at[slot, to], orecv.at[slot, z],
                osend.at[slot, d], orecv_sem.at[slot, d], at_z(z, c, plane, d),
            )
            copy.start()
            started.append(copy)

    spread(0)
    pass_on(0)
    for slot in range(SLOTS):
        settle(slot)
        for k in range(PLANES):
            attend(slot, k)
            if slot + 1 < SLOTS:
                if k == 1:
                    spread(slot + 1)
                if k == 3:
                    pass_on(slot + 1)
        give_back(slot)
    for slot in range(SLOTS):
        for d in range(1, PLANES):
            remote(
                opack.at[slot, 0], orecv.at[slot, 0],
                osend.at[slot, d], orecv_sem.at[slot, d], at_z(z, c, plane, d),
            ).wait_recv()
    for pair in range(HEADS // 2):
        parts = []
        for head in (2 * pair, 2 * pair + 1):
            src, slot = divmod(head, SLOTS)
            got = orecv[slot, src].astype(F32)
            parts.append(jnp.concatenate([got[:, :size], got[:, size:]], axis=0))
        att_ref[:, pair * 2 * size : (pair + 1) * 2 * size] = jnp.concatenate(parts, axis=1).astype(BF16)
    for copy in list(zcopies.values()) + started:
        copy.wait_send()


def forward_part(inputs, first_values, spans, ln1_gain, ln1_shift, w_query, b_query, w_key, w_value, b_value):
    rows, width = inputs.shape
    plane = lax.axis_size("blk") // PLANES
    lines = plane // 2
    size = width // HEADS
    half = rows // 2
    dma = pltpu.SemaphoreType.DMA
    return pl.pallas_call(
        functools.partial(forward_kernel, plane),
        name="forward",
        out_shape=(
            jax.ShapeDtypeStruct((rows, width), BF16),
            jax.ShapeDtypeStruct((rows, width), BF16),
            jax.ShapeDtypeStruct((SLOTS, PLANES, plane, rows + half, 2 * size), BF16),
            jax.ShapeDtypeStruct((SLOTS, PLANES, size, rows), F32),
            jax.ShapeDtypeStruct((SLOTS, PLANES, 8, rows), F32),
        ),
        in_specs=[VMEM, VMEM, SMEM] + [VMEM] * 7,
        out_specs=(VMEM,) * 5,
        scratch_shapes=[
            pltpu.VMEM((PLANES, SLOTS, rows + half, 2 * size), BF16),
            pltpu.VMEM((SLOTS, PLANES, half, 2 * size), BF16),
            pltpu.VMEM((SLOTS, PLANES, half, 2 * size), BF16),
            pltpu.VMEM((PLANES, plane * rows, rows), F32),
            dma((SLOTS, PLANES)), dma((SLOTS, PLANES)),
            dma((SLOTS, PLANES, lines)), dma((SLOTS, PLANES, lines)),
            dma((SLOTS, PLANES, lines)), dma((SLOTS, PLANES, lines)),
            dma((SLOTS, PLANES)), dma((SLOTS, PLANES)),
        ],
        compiler_params=pltpu.CompilerParams(
            collective_id=1, has_side_effects=True, vmem_limit_bytes=56 << 20
        ),
    )(
        inputs, first_values, spans, ln1_gain.reshape(1, -1), ln1_shift.reshape(1, -1),
        w_query, b_query.reshape(1, -1), w_key, w_value, b_value.reshape(1, -1),
    )


def layer_norm(values, gain_vector, shift_vector):
    average = jnp.mean(values, axis=-1, keepdims=True)
    centred = values - average
    variance = jnp.mean(centred * centred, axis=-1, keepdims=True)
    return centred * lax.rsqrt(variance + EPSILON) * gain_vector + shift_vector


def gelu_tanh(values):
    return (
        0.5 * values * (1.0 + jnp.tanh(GELU_COEF * (values + 0.044715 * values * values * values)))
    )


def key_alive(key_pos, bounds):
    return (key_pos < bounds[2]) | (key_pos >= bounds[1])


def backward_kernel(
    plane, mg_ref, all_ref, o_ref, lse_ref, spans_ref,
    dq_ref, dk_ref, dv_ref,
    dpack, drecv, masks, acc, part, cgot, xpart, xgot, ret, got,
    zsend, zrecv, csend, crecv, xsend, xrecv, rsend, rrecv,
):
    rows, width = mg_ref.shape
    size = width // HEADS
    lines = plane // 2
    length = rows * plane * PLANES
    half = rows // 2
    z, c = place(plane)
    column, core = c // 2, lax.rem(c, 2)
    greet(
        [at_z(z, c, plane, d) for d in range(1, PLANES)]
        + [at_x(z, c, plane, d) for d in range(1, lines)]
        + [at_core(z, c, plane)]
    )
    started = []
    for slot in range(SLOTS):
        for to in range(PLANES):
            cols = slice((to * SLOTS + slot) * size, (to * SLOTS + slot + 1) * size)
            dpack[to, slot] = jnp.concatenate([mg_ref[:half, cols], mg_ref[half:, cols]], axis=1)
        for d in (2, 1, 3):
            to = lax.rem(z + d, PLANES)
            copy = remote(
                dpack.at[to, slot], drecv.at[slot, z],
                zsend.at[slot, d], zrecv.at[slot, d], at_z(z, c, plane, d),
            )
            copy.start()
            started.append(copy)
        drecv[slot, z] = dpack[z, slot]
    for k in range(PLANES):
        masks[k] = position_masks(spans_ref, plane, length, c, k, rows)
    first, end = spans_ref[0, 0], length - spans_ref[0, 1]

    def arrive(slot):
        for d in range(1, PLANES):
            remote(
                dpack.at[0, slot], drecv.at[slot, z],
                zsend.at[slot, d], zrecv.at[slot, d], at_z(z, c, plane, d),
            ).wait_recv()

    def grads(slot, k):
        query = query_rows(all_ref[slot, k, c, rows:, :], True)
        grad = query_rows(drecv[slot, k], False)
        both = jnp.concatenate([query, grad], axis=0)
        turned = jnp.transpose(drecv[slot, k].astype(F32))
        turned = jnp.concatenate([turned[:size], turned[size:]], axis=1)
        delta = jnp.sum(turned * o_ref[slot, k], axis=0, keepdims=True)
        lse = lse_ref[slot, k, 0:1, :]
        query_grad = jnp.zeros((2 * size, rows), F32)
        for k2 in range(k, -1, -1):
            keys = all_ref[slot, k2, :, :rows, :].reshape(plane * rows, 2 * size)
            scores = dot(keys, query, NT)
            prob_grad = dot(keys, grad, NT)
            level = lse
            if k2 == k:
                scores = scores + masks[k]
            else:
                if k2 == 0:
                    index = lax.broadcasted_iota(jnp.int32, (plane * rows, 1), 0)
                    scores = scores + jnp.where(index < first, NEG_FILL, 0.0)
                if k == PLANES - 1:
                    position = k * plane * rows + c * rows + lax.broadcasted_iota(jnp.int32, (1, rows), 1)
                    level = jnp.where(position >= end, -NEG_FILL, lse)
            prob = jnp.exp(scores - level)
            score_grad = (prob * (prob_grad - delta)).astype(BF16)
            update = dot(jnp.concatenate([score_grad, prob.astype(BF16)], axis=1), both, NN)
            if k2 == k:
                acc[slot, k2] = update
            else:
                acc[slot, k2] += update
            query_grad = query_grad + dot(keys, score_grad, TN)
        packed = jnp.concatenate([query_grad[:size, :half], query_grad[:size, half:]], axis=0)
        ret[k, slot, rows:, :] = jnp.transpose(packed).astype(BF16)

    def mine(slot, k, col):
        return acc[slot, k, pl.ds(col * rows, rows), :]

    def reduce_core(slot):
        for line in range(lines):
            for k in range(PLANES):
                part[slot, line, k] = mine(slot, k, 2 * line + 1 - core).astype(BF16)
            copy = remote(
                part.at[slot, line], cgot.at[slot, line],
                csend.at[slot, line], crecv.at[slot, line], at_core(z, c, plane),
            )
            copy.start()
            started.append(copy)

    def reduce_line(slot):
        for line in range(lines):
            remote(
                part.at[slot, line], cgot.at[slot, line],
                csend.at[slot, line], crecv.at[slot, line], at_core(z, c, plane),
            ).wait_recv()
        for e in range(1, lines):
            line = lax.rem(column + e, lines)
            for k in range(PLANES):
                xpart[slot, e, k] = (
                    mine(slot, k, 2 * line + core) + cgot[slot, line, k].astype(F32)
                ).astype(BF16)
            copy = remote(
                xpart.at[slot, e], xgot.at[slot, e],
                xsend.at[slot, e], xrecv.at[slot, e], at_x(z, c, plane, e),
            )
            copy.start()
            started.append(copy)

    def reduce_end(slot):
        for e in range(1, lines):
            remote(
                xpart.at[slot, e], xgot.at[slot, e],
                xsend.at[slot, e], xrecv.at[slot, e], at_x(z, c, plane, e),
            ).wait_recv()
        for k in range(PLANES):
            total = mine(slot, k, c) + cgot[slot, column, k].astype(F32)
            for e in range(1, lines):
                total = total + xgot[slot, e, k].astype(F32)
            ret[k, slot, :rows, :] = total.astype(BF16)
        for d in (2, 1, 3):
            to = lax.rem(z + d, PLANES)
            copy = remote(
                ret.at[to, slot], got.at[slot, z],
                rsend.at[slot, d], rrecv.at[slot, d], at_z(z, c, plane, d),
            )
            copy.start()
            started.append(copy)
        got[slot, z] = ret[z, slot]

    for slot in range(SLOTS):
        arrive(slot)
        for k in range(PLANES):
            grads(slot, k)
            if slot and k == 1:
                reduce_line(slot - 1)
        if slot:
            reduce_end(slot - 1)
        reduce_core(slot)
    reduce_line(SLOTS - 1)
    reduce_end(SLOTS - 1)
    for slot in range(SLOTS):
        for d in range(1, PLANES):
            remote(
                ret.at[0, slot], got.at[slot, z],
                rsend.at[slot, d], rrecv.at[slot, d], at_z(z, c, plane, d),
            ).wait_recv()
    for pair in range(HEADS // 2):
        cols = slice(pair * 2 * size, (pair + 1) * 2 * size)
        keys, values, queries = [], [], []
        for head in (2 * pair, 2 * pair + 1):
            src, slot = divmod(head, SLOTS)
            block = got[slot, src].astype(F32)
            keys.append(block[:rows, :size])
            values.append(block[:rows, size:])
            queries.append(jnp.concatenate([block[rows:, :size], block[rows:, size:]], axis=0))
        dq_ref[:, cols] = jnp.concatenate(queries, axis=1).astype(BF16)
        dk_ref[:, cols] = jnp.concatenate(keys, axis=1).astype(BF16)
        dv_ref[:, cols] = jnp.concatenate(values, axis=1).astype(BF16)
    for copy in started:
        copy.wait_send()


def backward_part(mixed_grad, all_blocks, mixed, lse, spans):
    rows, width = mixed_grad.shape
    plane = lax.axis_size("blk") // PLANES
    lines = plane // 2
    size = width // HEADS
    half = rows // 2
    dma = pltpu.SemaphoreType.DMA
    return pl.pallas_call(
        functools.partial(backward_kernel, plane),
        name="backward",
        out_shape=(jax.ShapeDtypeStruct((rows, width), BF16),) * 3,
        in_specs=[VMEM, VMEM, VMEM, VMEM, SMEM],
        out_specs=(VMEM,) * 3,
        scratch_shapes=[
            pltpu.VMEM((PLANES, SLOTS, half, 2 * size), BF16),
            pltpu.VMEM((SLOTS, PLANES, half, 2 * size), BF16),
            pltpu.VMEM((PLANES, plane * rows, rows), F32),
            pltpu.VMEM((SLOTS, PLANES, plane * rows, 2 * size), F32),
            pltpu.VMEM((SLOTS, lines, PLANES, rows, 2 * size), BF16),
            pltpu.VMEM((SLOTS, lines, PLANES, rows, 2 * size), BF16),
            pltpu.VMEM((SLOTS, lines, PLANES, rows, 2 * size), BF16),
            pltpu.VMEM((SLOTS, lines, PLANES, rows, 2 * size), BF16),
            pltpu.VMEM((PLANES, SLOTS, rows + half, 2 * size), BF16),
            pltpu.VMEM((SLOTS, PLANES, rows + half, 2 * size), BF16),
            dma((SLOTS, PLANES)), dma((SLOTS, PLANES)),
            dma((SLOTS, lines)), dma((SLOTS, lines)),
            dma((SLOTS, lines)), dma((SLOTS, lines)),
            dma((SLOTS, PLANES)), dma((SLOTS, PLANES)),
        ],
        compiler_params=pltpu.CompilerParams(
            collective_id=2, has_side_effects=True, vmem_limit_bytes=56 << 20
        ),
    )(mixed_grad, all_blocks, mixed, lse, spans)


def body(
    inputs,
    first_values,
    spans,
    ln1_gain,
    ln1_shift,
    w_query,
    b_query,
    w_key,
    w_value,
    b_value,
    w_out,
    b_out,
    ln2_gain,
    ln2_shift,
    w_up,
    b_up,
    w_down,
    b_down,
    out_grad,
):
    row_count = inputs.shape[0]
    model_width = inputs.shape[1]
    half_width = model_width // 2
    block_count = lax.axis_size("blk")
    length = row_count * block_count
    my_index = lax.axis_index("blk")
    start_row = my_index * row_count
    positions = start_row + jnp.arange(row_count, dtype=jnp.int32)
    long_end = length - spans[0, 1]
    bounds = (spans[0, 0], long_end, long_end - spans[0, 2])
    source = inputs.astype(jnp.float32)
    attended_low, normed_low, all_blocks, mixed, lse = forward_part(
        inputs, first_values, spans, ln1_gain, ln1_shift, w_query, b_query, w_key, w_value, b_value
    )
    ln1_back = jax.vjp(layer_norm, source, ln1_gain, ln1_shift)[1]
    hidden = source + jnp.dot(attended_low, w_out, preferred_element_type=jnp.float32) + b_out
    normed2, ln2_back = jax.vjp(layer_norm, hidden, ln2_gain, ln2_shift)
    normed2_low = normed2.astype(jnp.bfloat16)
    upper = jnp.dot(normed2_low, w_up, preferred_element_type=jnp.float32) + b_up
    active, gelu_back = jax.vjp(gelu_tanh, upper)
    active_low = active.astype(jnp.bfloat16)
    result = hidden + jnp.dot(active_low, w_down, preferred_element_type=jnp.float32) + b_down
    alive_rows = key_alive(positions, bounds)
    grad_down = out_grad * alive_rows.astype(jnp.bfloat16)[:, None]
    g_w_down = jnp.einsum("tf,td->fd", active_low, grad_down, preferred_element_type=jnp.float32)
    g_b_down = jnp.sum(grad_down.astype(jnp.float32), axis=0)
    active_grad = jnp.einsum("td,fd->tf", grad_down, w_down, preferred_element_type=jnp.float32)
    upper_grad = gelu_back(active_grad)[0].astype(jnp.bfloat16)
    g_w_up = jnp.einsum("tc,tf->cf", normed2_low, upper_grad, preferred_element_type=jnp.float32)
    g_b_up = jnp.sum(upper_grad.astype(jnp.float32), axis=0)
    normed2_grad = jnp.einsum("tf,cf->tc", upper_grad, w_up, preferred_element_type=jnp.float32)
    hidden_norm_grad, g_ln2_gain, g_ln2_shift = ln2_back(normed2_grad)
    hidden_grad = grad_down.astype(jnp.float32) + hidden_norm_grad
    branch_grad = hidden_grad.astype(jnp.bfloat16)
    g_w_out = jnp.einsum("tc,td->cd", attended_low, branch_grad, preferred_element_type=jnp.float32)
    g_b_out = jnp.sum(branch_grad.astype(jnp.float32), axis=0)
    mixed_grad = jnp.einsum(
        "td,cd->tc", branch_grad, w_out, preferred_element_type=jnp.float32
    ).astype(jnp.bfloat16)
    query_grad, key_grad_low, value_grad_low = backward_part(mixed_grad, all_blocks, mixed, lse, spans)
    scaled_grad = query_grad * jnp.bfloat16(0.125)
    fresh_grad = value_grad_low[:, :half_width]
    grad_first_values = value_grad_low[:, half_width:]
    g_w_query = jnp.einsum("tc,td->cd", normed_low, scaled_grad, preferred_element_type=jnp.float32)
    g_b_query = jnp.sum(scaled_grad.astype(jnp.float32), axis=0)
    g_w_key = jnp.einsum("tc,td->cd", normed_low, key_grad_low, preferred_element_type=jnp.float32)
    g_w_value = jnp.einsum("tc,td->cd", normed_low, fresh_grad, preferred_element_type=jnp.float32)
    g_b_value = jnp.sum(fresh_grad.astype(jnp.float32), axis=0)
    normed_grad = (
        jnp.einsum("td,cd->tc", scaled_grad, w_query, preferred_element_type=jnp.float32)
        + jnp.einsum("td,cd->tc", key_grad_low, w_key, preferred_element_type=jnp.float32)
        + jnp.einsum("td,cd->tc", fresh_grad, w_value, preferred_element_type=jnp.float32)
    )
    source_grad, g_ln1_gain, g_ln1_shift = ln1_back(normed_grad)
    grad_inputs = hidden_grad + source_grad
    vector_parts = (
        g_ln1_gain,
        g_ln1_shift,
        g_b_query,
        g_b_value,
        g_b_out,
        g_ln2_gain,
        g_ln2_shift,
        g_b_up,
        g_b_down,
    )
    vector_total = lax.psum(jnp.concatenate(vector_parts, axis=0), ("grp", "blk"))
    offsets = [0]
    for member in vector_parts:
        offsets.append(offsets[-1] + member.shape[0])
    summed_vectors = [
        vector_total[offsets[place] : offsets[place + 1]] for place in range(len(vector_parts))
    ]
    matrices = (g_w_query, g_w_key, g_w_value, g_w_out, g_w_up, g_w_down)
    shard_sums = (
        lax.psum_scatter(
            matrices[0].astype(jnp.bfloat16), "blk", scatter_dimension=0, tiled=True
        ).astype(jnp.float32),
        lax.psum_scatter(
            matrices[1].astype(jnp.bfloat16), "blk", scatter_dimension=0, tiled=True
        ).astype(jnp.float32),
        lax.psum_scatter(
            matrices[2].astype(jnp.bfloat16), "blk", scatter_dimension=0, tiled=True
        ).astype(jnp.float32),
        lax.psum_scatter(
            matrices[3].astype(jnp.bfloat16), "blk", scatter_dimension=0, tiled=True
        ).astype(jnp.float32),
        lax.psum_scatter(
            matrices[4].astype(jnp.bfloat16), "blk", scatter_dimension=0, tiled=True
        ).astype(jnp.float32),
        lax.psum_scatter(
            matrices[5].astype(jnp.bfloat16), "blk", scatter_dimension=0, tiled=True
        ).astype(jnp.float32),
    )
    shard_sums = (
        lax.psum(shard_sums[0].astype(jnp.bfloat16), "grp").astype(jnp.float32),
        lax.psum(shard_sums[1].astype(jnp.bfloat16), "grp").astype(jnp.float32),
        lax.psum(shard_sums[2].astype(jnp.bfloat16), "grp").astype(jnp.float32),
        lax.psum(shard_sums[3].astype(jnp.bfloat16), "grp").astype(jnp.float32),
        lax.psum(shard_sums[4].astype(jnp.bfloat16), "grp").astype(jnp.float32),
        lax.psum(shard_sums[5].astype(jnp.bfloat16), "grp").astype(jnp.float32),
    )
    return (
        result,
        grad_inputs,
        grad_first_values,
        summed_vectors[0],
        summed_vectors[1],
        shard_sums[0],
        summed_vectors[2],
        shard_sums[1],
        shard_sums[2],
        summed_vectors[3],
        shard_sums[3],
        summed_vectors[4],
        summed_vectors[5],
        summed_vectors[6],
        shard_sums[4],
        summed_vectors[7],
        shard_sums[5],
        summed_vectors[8],
    )


def solution(mesh):
    placed = (
        P(("grp", "blk"), None),
        P(("grp", "blk"), None),
        P("grp", None),
        P(),
        P(),
        P(),
        P(),
        P(),
        P(),
        P(),
        P(),
        P(),
        P(),
        P(),
        P(),
        P(),
        P(),
        P(),
        P(("grp", "blk"), None),
    )
    return jax.shard_map(
        body,
        mesh=mesh,
        in_specs=placed,
        out_specs=(
            P(("grp", "blk"), None),
            P(("grp", "blk"), None),
            P(("grp", "blk"), None),
            P(),
            P(),
            P("blk", None),
            P(),
            P("blk", None),
            P("blk", None),
            P(),
            P("blk", None),
            P(),
            P(),
            P(),
            P("blk", None),
            P(),
            P("blk", None),
            P(),
        ),
        check_vma=False,
    )
```

time: 803 us -> 617 us (0.77)
  blocking collectives: 238 us -> 49.7 us
  matrix products: 186 us -> 50 us
  Pallas kernels: 0 us -> 123 us
  waiting for transfers between devices: 232 us -> 332 us
  local copies, waits for them, and re-layouts: 78.5 us -> 22.5 us
  other arithmetic: 37.5 us -> 12.8 us
    all_gather x2 -> x0, blocking collectives: 189 us -> none  [the longest x1 169 us: body(): lax.all_gather(row_delta, 'blk', axis=0, tiled=True)]
    dot_general x31 -> x0, matrix products: 146 us -> none  [the longest x8 57.7 us: query_compute(): jnp.einsum('hqk,qhd->khd', score_grads, query_block, preferred_element_ty...]
    pallas_call x0 -> x2, Pallas kernels: none -> 123 us  [the longest x1 65.8 us: forward_part(): pl.pallas_call(functools.partial(forward_kernel, plane), name='forward',...]
    all_gather x4 -> x0, waiting for transfers between devices: 112 us -> none  [the longest x1 57.8 us: body(): key_piece = lax.all_gather(key_low, 'blk', axis=0, tiled=True)]
    reduce_scatter x1, waiting for transfers between devices: 0.02 us -> 78.4 us  [body(): lax.psum_scatter(matrices[4].astype(jnp.bfloat16), 'blk', scatter_dimensi...]
    reduce_scatter x1, waiting for transfers between devices: 60.7 us -> 0.02 us  [body(): lax.psum_scatter(matrices[1].astype(jnp.bfloat16), 'blk', scatter_dimensi...]
    reduce_scatter x1, waiting for transfers between devices: 0.02 us -> 60.7 us  [body(): lax.psum_scatter(matrices[0].astype(jnp.bfloat16), 'blk', scatter_dimensi...]
    reduce_scatter x1, waiting for transfers between devices: 18.6 us -> 78.9 us  [body(): lax.psum_scatter(matrices[5].astype(jnp.bfloat16), 'blk', scatter_dimensi...]
  transfers between devices with their start and end apart: 11 -> 7, of which waited for: 6 -> 6; matrix products, arithmetic and copies ran while one was open for 35% -> 8% of each run, Pallas kernels for 0% -> 0%
where the time goes in v1:
time: 617 us; the launch traced here: 607 us
  waiting for transfers between devices  332 us (54%)
  Pallas kernels  123 us (20%)
  matrix products  50 us (8%)
  blocking collectives  49.7 us (8%)
  local copies, waits for them, and re-layouts  22.5 us (4%)
  between operations  16.1 us (3%)
  other arithmetic  12.8 us (2%)
    reduce_scatter x1, waiting for transfers between devices, body(): lax.psum_scatter(matrices[5].astype(jnp.bfloat16), 'blk', scatter_dimensi...  78.9 us
    reduce_scatter x1, waiting for transfers between devices, body(): lax.psum_scatter(matrices[4].astype(jnp.bfloat16), 'blk', scatter_dimensi...  78.4 us
    pallas_call x1, Pallas kernels, forward_part(): pl.pallas_call(functools.partial(forward_kernel, plane), name='forward',...  65.8 us
    reduce_scatter x1, waiting for transfers between devices, body(): lax.psum_scatter(matrices[0].astype(jnp.bfloat16), 'blk', scatter_dimensi...  60.7 us
    pallas_call x1, Pallas kernels, backward_part(): pl.pallas_call(functools.partial(backward_kernel, plane), name='backward'...  57.6 us
    reduce_scatter x1, waiting for transfers between devices, body(): lax.psum_scatter(matrices[2].astype(jnp.bfloat16), 'blk', scatter_dimensi...  49.2 us
    psum x1, blocking collectives, body(): lax.psum(jnp.concatenate(vector_parts, axis=0), ('grp', 'blk'))  40.7 us
    reduce_scatter x1, waiting for transfers between devices, body(): lax.psum_scatter(matrices[3].astype(jnp.bfloat16), 'blk', scatter_dimensi...  37 us
  transfers between devices with their start and end apart: 7, of which 6 were waited for; matrix products, arithmetic and copies ran while one was open for 8% of the time, Pallas kernels for 0%

profile of v1, /device:TPU:0, one launch (start us, length us, event | category | flops | bytes accessed | tf_op | source)
XLA Modules:
  0.0 607.0 jit_solution(1899264780989363851)
XLA Ops:
  7.3 1.4 reshape.124.g_ref
  8.6 1.3 reshape.125.s_ref
  9.9 1.3 reshape.126.bq_ref
  11.2 1.2 reshape.127.bv_ref
  12.4 1.3 fusion.40
  13.8 65.8 %forward.1 = (bf16[256,768]{1,0:T(8,128)(2,1)}, bf16[256,768]{1,0:T(8,128)(2,1)}, bf16[3,4,4,384,128]{4,3,2,1,0:T(8,128)(2,1)}, f32[3,4,64,256]{3,2,1,0:T(8,128)}, f32[3,4,8,256]{3,2,1,0:T(8,128)}) custom-call(bf16[256,768]{1,0:T(8,128)(2,1)} %x_ref.1, bf16[256,384]{1,0:T(8,128)(2,1)} %fv_ref.1, s32[1,3]{1,0:T(1,128)} %spans_ref.3, ...), custom_call_target="tpu_custom_call" | custom-call | tf_op jit(solution)/shard_map/forward/pallas_call | solution.py:280
  79.6 1.6 fusion.41
  81.2 0.2 multiply_reduce_fusion.2
  82.8 4.0 convolution_add_fusion
  86.8 7.8 %convert_reduce_fusion = (f32[3072]{0:T(1024)}, bf16[256,3072]{1,0:T(8,128)(2,1)S(1)}) fusion(f32[256,3072]{1,0:T(8,128)S(1)} %convolution_add_fusion, bf16[3072,768]{1,0:T(8,128)(2,1)} %param.35, bf16[256,768]{1,0:T(8,128)(2,1)S(1)} %copy-done.6, bf16[256]{0:T(256)(128)(2,1)S(1)} %or_convert_fusion), kind=kOutput, calls=%fused_computation.13 | convolution fusion | flops 1228600320 | bytes 9843200 | tf_op jit(solution)/shard_map/td,fd->tf/dot_general | solution.py:574
  94.6 2.2 multiply_reduce_fusion
  96.8 0.3 fusion.38
  97.2 0.2 convert_reduce_fusion.3
  97.4 0.3 copy-done.16
  97.7 0.7 copy-done.4
  98.5 1.2 convolution_convert_fusion.6.mg_ref
  99.7 57.6 %backward.1 = (bf16[256,768]{1,0:T(8,128)(2,1)}, bf16[256,768]{1,0:T(8,128)(2,1)}, bf16[256,768]{1,0:T(8,128)(2,1)}) custom-call(bf16[256,768]{1,0:T(8,128)(2,1)} %convolution_convert_fusion.6.mg_ref, bf16[3,4,4,384,128]{4,3,2,1,0:T(8,128)(2,1)} %get-tuple-element.27.all_ref, f32[3,4,64,256]{3,2,1,0:T(8,128)} %get-tuple-element.28.o_ref, ...), custom_call_target="tpu_custom_call" | custom-call | tf_op jit(solution)/shard_map/backward/pallas_call | solution.py:499
  157.4 2.6 convolution_convert_fusion.3
  160.1 2.6 convolution_convert_fusion.2
  162.8 2.6 convolution_convert_fusion.4
  165.4 0.0 reduce-scatter.15.cloned.1.call-start
  165.4 5.2 convolution_convert_fusion.1
  170.6 0.0 reduce-scatter.17.cloned.1.call-start
  170.7 0.6 copy-done.19
  171.3 6.5 %convolution_convert_fusion = bf16[3072,768]{1,0:T(8,128)(2,1)} fusion(bf16[256,768]{1,0:T(8,128)(2,1)} %param.37, bf16[256]{0:T(256)(128)(2,1)S(1)} %copy-done.19, f32[256,3072]{1,0:T(8,128)} %copy-done.25), kind=kOutput, calls=%fused_computation | convolution fusion | flops 1217593344 | bytes 8258048 | tf_op jit(solution)/shard_map/tf,td->fd/dot_general | solution.py:572
  177.7 0.0 reduce-scatter.11.cloned.1.call-start
  177.8 2.3 convolution_convert_fusion.5
  180.1 0.2 all-reduce.3.cloned.1.call-start
  180.3 2.7 fusion.18
  183.0 0.1 convert_reduce_fusion.1
  183.1 0.1 convert_reduce_fusion.4
  183.2 1.0 convert_reduce_fusion.5
  184.3 2.2 convolution_add_fusion.2
  186.6 0.6 fusion.36
  187.1 0.5 fusion.15
  187.6 1.3 constant_dynamic-update-slice_fusion.8
  188.9 1.3 constant_dynamic-update-slice_fusion.7
  190.2 1.3 constant_dynamic-update-slice_fusion.6
  191.5 1.3 constant_dynamic-update-slice_fusion.5
  192.8 1.3 constant_dynamic-update-slice_fusion.4
  194.1 1.3 constant_dynamic-update-slice_fusion.3
  195.4 1.3 constant_dynamic-update-slice_fusion.2
  196.7 1.3 constant_dynamic-update-slice_fusion.1
  198.0 1.3 convert_reduce_fusion.2
  199.4 1.3 constant_dynamic-update-slice_fusion
  200.7 40.7 %psum.49 = f32[8832]{0:T(1024)S(1)} all-reduce(f32[8832]{0:T(1024)} %constant_dynamic-update-slice_fusion), channel_id=1, replica_groups=mesh['grp'=2,'blk'=16] {'grp','blk'}, use_global_device_ids=true, to_apply=%region_17.0 | all-reduce | flops 8832 | bytes 70656 | tf_op jit(solution)/shard_map/psum | solution.py:614
  241.4 37.0 %reduce-scatter.13.cloned.1.call-done = bf16[48,768]{1,0:T(8,128)(2,1)} async-done(((bf16[768,768]{1,0:T(8,128)(2,1)}), bf16[48,768]{1,0:T(8,128)(2,1)}) %reduce-scatter.13.cloned.1.call-update) | async-done | bytes 73744 | tf_op jit(solution)/shard_map/reduce_scatter | solution.py:632
  278.4 60.7 %reduce-scatter.7.cloned.1.call-done = bf16[48,768]{1,0:T(8,128)(2,1)} async-done(((bf16[768,768]{1,0:T(8,128)(2,1)}), bf16[48,768]{1,0:T(8,128)(2,1)}) %reduce-scatter.7.cloned.1.call-update) | async-done | bytes 73744 | tf_op jit(solution)/shard_map/reduce_scatter | solution.py:623
  339.1 78.4 %reduce-scatter.15.cloned.1.call-done = bf16[48,3072]{1,0:T(8,128)(2,1)} async-done(((bf16[768,3072]{1,0:T(8,128)(2,1)}), bf16[48,3072]{1,0:T(8,128)(2,1)}) %reduce-scatter.15.cloned.1.call-update) | async-done | bytes 294928 | tf_op jit(solution)/shard_map/reduce_scatter | solution.py:635
  417.5 78.9 %reduce-scatter.17.cloned.1.call-done = bf16[192,768]{1,0:T(8,128)(2,1)} async-done(((bf16[3072,768]{1,0:T(8,128)(2,1)}), bf16[192,768]{1,0:T(8,128)(2,1)}) %reduce-scatter.17.cloned.1.call-update) | async-done | bytes 294928 | tf_op jit(solution)/shard_map/reduce_scatter | solution.py:638
  496.4 0.6 fusion.39
  497.0 0.6 slice.59
  497.6 0.6 slice.55
  498.2 0.7 slice.42
  498.9 6.2 %fusion.7 = f32[256,768]{1,0:T(8,128)} fusion(f32[256,768]{1,0:T(8,128)S(1)} %get-tuple-element.65, bf16[3072,768]{1,0:T(8,128)(2,1)} %param.35, f32[768]{0:T(1024)} %param.36, f32[256,3072]{1,0:T(8,128)} %copy-done.25), kind=kOutput, calls=%fused_computation.24 | convolution fusion | flops 1215430656 | bytes 9440256 | tf_op jit(solution)/shard_map/dot_general | solution.py:569
  505.0 49.2 %reduce-scatter.11.cloned.1.call-done = bf16[48,384]{1,0:T(8,128)(2,1)} async-done(((bf16[768,384]{1,0:T(8,128)(2,1)}), bf16[48,384]{1,0:T(8,128)(2,1)}) %reduce-scatter.11.cloned.1.call-update) | async-done | bytes 36880 | tf_op jit(solution)/shard_map/reduce_scatter | solution.py:629
  554.3 9.0 %psum.52 = bf16[48,384]{1,0:T(8,128)(2,1)S(1)} all-reduce(bf16[48,384]{1,0:T(8,128)(2,1)} %reduce-scatter.11.cloned.1.call-done), channel_id=1, replica_groups=mesh['grp'=2,'blk'=16] {'grp'}, use_global_device_ids=true, to_apply=%region_23.0 | all-reduce | flops 18432 | bytes 73728 | tf_op jit(solution)/shard_map/psum | solution.py:645
  563.3 0.6 convert_element_type.106
  563.9 27.7 %all-reduce.3.cloned.1.call-done = (bf16[48,768]{1,0:T(8,128)(2,1)}, bf16[48,768]{1,0:T(8,128)(2,1)}, bf16[48,768]{1,0:T(8,128)(2,1)}, bf16[48,3072]{1,0:T(8,128)(2,1)}, bf16[192,768]{1,0:T(8,128)(2,1)}) async-done(((bf16[48,768]{1,0:T(8,128)(2,1)}, bf16[48,768]{1,0:T(8,128)(2,1)}, bf16[48,768]{1,0:T(8,128)(2,1)}, bf16[48,3072]{1,0:T(8,128)(2,1)}, bf16[192,768]{1,0:T(8,128)(2,1)}), ...) | async-done | bytes 811024 | tf_op jit(solution)/shard_map/psum | solution.py:643
  591.6 1.8 convert_element_type.110
  593.5 1.8 convert_element_type.112
  595.3 1.6 convert_element_type.102
  596.8 1.6 convert_element_type.104
  598.4 1.6 convert_element_type.108
  (74 shorter events, 0.5 us)
Async XLA Ops:
  7.2 72.4 %copy-start = (bf16[768,768]{1,0:T(8,128)(2,1)S(1)}, bf16[768,768]{1,0:T(8,128)(2,1)}, u32[]{:S(2)}) copy-start(bf16[768,768]{1,0:T(8,128)(2,1)} %param.29) | copy-start | bytes 3538948
  7.2 72.4 %copy-start.1 = (bf16[256,768]{1,0:T(8,128)(2,1)S(1)}, bf16[256,768]{1,0:T(8,128)(2,1)}, u32[]{:S(2)}) copy-start(bf16[256,768]{1,0:T(8,128)(2,1)} %x_ref.1) | copy-start | bytes 1179652
  7.2 72.4 %copy-start.21 = (f32[768]{0:T(1024)S(1)}, f32[768]{0:T(1024)}, u32[]{:S(2)}) copy-start(f32[768]{0:T(1024)} %param.30) | copy-start | bytes 9220
  7.2 234.2 %reduce-scatter.9.cloned.1.call-start = ((), (), s32[]{:S(2)}) async-start(), calls=%async_computation.7 | async-start | bytes 1253376 | tf_op jit(solution)/shard_map/reduce_scatter | solution.py:626
  13.7 69.0 %copy-start.11 = (f32[768]{0:T(1024)S(1)}, f32[768]{0:T(1024)}, u32[]{:S(2)}) copy-start(f32[768]{0:T(1024)} %param.31) | copy-start | bytes 9220
  13.7 69.0 %copy-start.12 = (f32[768]{0:T(1024)S(1)}, f32[768]{0:T(1024)}, u32[]{:S(2)}) copy-start(f32[768]{0:T(1024)} %param.32) | copy-start | bytes 9220
  13.7 69.0 %copy-start.24 = (f32[3072]{0:T(1024)S(1)}, f32[3072]{0:T(1024)}, u32[]{:S(2)}) copy-start(f32[3072]{0:T(1024)} %param.34) | copy-start | bytes 36868
  81.4 15.4 %copy-start.14 = (f32[256]{0:T(256)}, f32[256]{0:T(256)S(1)}, u32[]{:S(2)}) copy-start(f32[256]{0:T(256)S(1)} %fusion.31) | copy-start | bytes 3076
  82.8 14.4 %copy-start.18 = (bf16[256]{0:T(256)(128)(2,1)}, bf16[256]{0:T(256)(128)(2,1)S(1)}, u32[]{:S(2)}) copy-start(bf16[256]{0:T(256)(128)(2,1)S(1)} %or_convert_fusion) | copy-start | bytes 1540
  82.8 4.0 copy-start.6
  82.8 11.8 %slice-start = ((s8[4718592]{0:T(1024)(128)(4,1)}), s8[4194304]{0:T(1024)(128)(4,1)S(1)}, s32[]{:S(2)}) async-start(s8[4718592]{0:T(1024)(128)(4,1)} %bitcast.22), calls=%async_computation.13 | async-start | bytes 8388608
  86.8 7.8 %copy-start.25 = (f32[256,3072]{1,0:T(8,128)}, f32[256,3072]{1,0:T(8,128)S(1)}, u32[]{:S(2)}) copy-start(f32[256,3072]{1,0:T(8,128)S(1)} %convolution_add_fusion) | copy-start | bytes 9437188
  86.8 7.8 %slice-start.1 = ((s8[4718592]{0:T(1024)(128)(4,1)}), s8[524288]{0:T(1024)(128)(4,1)S(1)}, s32[]{:S(2)}) async-start(s8[4718592]{0:T(1024)(128)(4,1)} %bitcast.22), calls=%async_computation.14 | async-start | bytes 1048576
  94.6 2.2 copy-start.10
  97.2 0.6 copy-start.16
  97.7 0.7 copy-start.4
  99.7 57.6 %copy-start.3 = (bf16[256,768]{1,0:T(8,128)(2,1)S(1)}, bf16[256,768]{1,0:T(8,128)(2,1)}, u32[]{:S(2)}) copy-start(bf16[256,768]{1,0:T(8,128)(2,1)} %get-tuple-element.33) | copy-start | bytes 1179652
  157.3 5.5 copy-start.2
  160.0 118.4 %reduce-scatter.13.cloned.1.call-start = ((), (), s32[]{:S(2)}) async-start(), calls=%async_computation.9 | async-start | bytes 1253376 | tf_op jit(solution)/shard_map/reduce_scatter | solution.py:632
  162.7 176.4 %reduce-scatter.7.cloned.1.call-start = ((), (), s32[]{:S(2)}) async-start(), calls=%async_computation.6 | async-start | bytes 1253376 | tf_op jit(solution)/shard_map/reduce_scatter | solution.py:623
  165.4 252.1 %reduce-scatter.15.cloned.1.call-start = ((), (), s32[]{:S(2)}) async-start(), calls=%async_computation.10 | async-start | bytes 5013504 | tf_op jit(solution)/shard_map/reduce_scatter | solution.py:635
  170.6 0.7 copy-start.19
  170.6 325.7 %reduce-scatter.17.cloned.1.call-start = ((), (), s32[]{:S(2)}) async-start(), calls=%async_computation.11 | async-start | bytes 5013504 | tf_op jit(solution)/shard_map/reduce_scatter | solution.py:638
  177.7 376.5 %reduce-scatter.11.cloned.1.call-start = ((), (), s32[]{:S(2)}) async-start(), calls=%async_computation.8 | async-start | bytes 626688 | tf_op jit(solution)/shard_map/reduce_scatter | solution.py:629
  180.1 6.5 %copy-start.13 = (f32[768]{0:T(1024)S(1)}, f32[768]{0:T(1024)}, u32[]{:S(2)}) copy-start(f32[768]{0:T(1024)} %param.22) | copy-start | bytes 9220
  180.1 411.6 %all-reduce.3.cloned.1.call-start = ((), (), s32[]{:S(2)}) async-start(), calls=%async_computation.12 | async-start | bytes 1622016 | tf_op jit(solution)/shard_map/psum | solution.py:643
  183.1 3.4 copy-start.5
  183.1 3.4 copy-start.8
  184.3 9.8 %copy-start.23 = (f32[768]{0:T(1024)S(1)}, f32[768]{0:T(1024)}, u32[]{:S(2)}) copy-start(f32[768]{0:T(1024)} %get-tuple-element.34) | copy-start | bytes 9220
  184.3 11.1 %copy-start.22 = (f32[768]{0:T(1024)S(1)}, f32[768]{0:T(1024)}, u32[]{:S(2)}) copy-start(f32[768]{0:T(1024)} %get-tuple-element.38) | copy-start | bytes 9220
  184.3 12.4 %copy-start.15 = (f32[3072]{0:T(1024)S(1)}, f32[3072]{0:T(1024)}, u32[]{:S(2)}) copy-start(f32[3072]{0:T(1024)} %get-tuple-element.68) | copy-start | bytes 36868
  184.3 13.7 %copy-start.7 = (bf16[256,768]{1,0:T(8,128)(2,1)S(1)}, bf16[256,768]{1,0:T(8,128)(2,1)}, u32[]{:S(2)}) copy-start(bf16[256,768]{1,0:T(8,128)(2,1)} %param.37) | copy-start | bytes 1179652
  184.3 13.7 %copy-start.17 = (f32[256]{0:T(256)S(1)}, f32[256]{0:T(256)}, u32[]{:S(2)}) copy-start(f32[256]{0:T(256)} %copy-done.16) | copy-start | bytes 3076
  184.3 13.7 %copy-start.20 = (bf16[256]{0:T(256)(128)(2,1)S(1)}, bf16[256]{0:T(256)(128)(2,1)}, u32[]{:S(2)}) copy-start(bf16[256]{0:T(256)(128)(2,1)} %copy-done.18) | copy-start | bytes 1540
  187.1 311.1 %copy-start.9 = (bf16[256,768]{1,0:T(8,128)(2,1)S(1)}, bf16[256,768]{1,0:T(8,128)(2,1)}, u32[]{:S(2)}) copy-start(bf16[256,768]{1,0:T(8,128)(2,1)} %get-tuple-element.32) | copy-start | bytes 1179652
Sparse Core Ops, SparseCore 0:
  160.1 57.4 reduce-scatter.8
  221.2 57.1 reduce-scatter.12
  282.1 57.0 reduce-scatter.6
  342.9 74.5 reduce-scatter.14
  421.7 74.6 reduce-scatter.16
  500.3 53.8 reduce-scatter.10
  557.0 34.5 all-reduce.2
